TPU v7x, 32 devices: a whole 2x2x4 slice. The times are simulated.
32 devices in a mesh: rep: 8 (over y, x, core), fsdp: 4 (over z).
Axes of the slice: x: 2, y: 2, z: 4, core: 2. Of those that a mesh axis runs over, the one named last changes fastest.
Arguments:
- tokens: bfloat16 [8, 1024, 4096], P('rep', 'fsdp'), may hold values from -90 to 90
- cotangent: bfloat16 [8, 1024, 2048], P('rep', 'fsdp'), may hold values from -6 to 6
- w_slow: bfloat16 [8, 4096, 2048], P('rep', 'fsdp'), may hold values from -6 to 6
- drift: bfloat16 [8, 4096, 2048], P('rep', 'fsdp'), may hold values from -4 to 4
- momentum: bfloat16 [8, 4096, 2048], P('rep', 'fsdp'), may hold values from -4 to 4
- partner: int32 [8], replicated, may hold values from 0 to 7, as said below
Outputs:
- momentum_new: bfloat16 [8, 4096, 2048], P('rep', 'fsdp')
- weights_new: bfloat16 [8, 4096, 2048], P('rep', 'fsdp')
Inputs may be any that keep to these rules, and one draw needn't show every extreme that they name: partner[partner[r]] == r and partner[r] != r for every replica r.
All inputs are finite; a program needn't handle non-finite values.
Results may differ from a plain program's by a relative error of at most 0.013.
Values may be sent and summed in bfloat16 or wider, within the bound.
A program may use at most 128 MiB of HBM per device.

v0:
```python
import jax
import jax.numpy as jnp
from jax import lax
from jax.sharding import PartitionSpec as P

D = 4096
DO = 2048


def mixing_term(drift_part, slow_part):
    return (
        0.5 * (0.7 * drift_part.astype(jnp.float32) - 0.3 * slow_part.astype(jnp.float32))
    ).astype(jnp.bfloat16)


def on_device(tokens, cotangent, w_slow, drift, momentum, partner):
    local_x = tokens[0]
    local_g = cotangent[0]
    grad = lax.psum_scatter(
        lax.dot_general(
            local_x, local_g, (((0,), (0,)), ((), ())), preferred_element_type=jnp.float32
        ).astype(jnp.bfloat16),
        "fsdp",
        scatter_dimension=0,
        tiled=True,
    ).astype(jnp.float32)
    squares = lax.psum(jnp.sum(grad * grad), "fsdp")
    scale = jnp.sqrt(squares / (D * DO) + 1e-06)
    owned_drift, owned_slow = (
        lax.all_to_all(drift, "rep", split_axis=1, concat_axis=0, tiled=True),
        lax.all_to_all(w_slow, "rep", split_axis=1, concat_axis=0, tiled=True),
    )
    mate_drift = jnp.take(owned_drift, partner, axis=0)
    mate_slow = jnp.take(owned_slow, partner, axis=0)
    back_drift, back_slow = (
        lax.all_to_all(mate_drift, "rep", split_axis=0, concat_axis=1, tiled=True),
        lax.all_to_all(mate_slow, "rep", split_axis=0, concat_axis=1, tiled=True),
    )
    partner_mix = mixing_term(back_drift, back_slow)
    own_slow = w_slow.astype(jnp.float32)
    moment = (
        0.5 * momentum.astype(jnp.float32)
        + 0.35 * drift.astype(jnp.float32)
        + 0.15 * own_slow
        + partner_mix.astype(jnp.float32)
    )
    weights = own_slow - moment - 0.5 * (grad / scale)[None]
    return (moment.astype(jnp.bfloat16), weights.astype(jnp.bfloat16))


def solution(mesh):
    return jax.shard_map(
        on_device,
        mesh=mesh,
        in_specs=(
            P("rep", "fsdp", None),
            P("rep", "fsdp", None),
            P("rep", "fsdp", None),
            P("rep", "fsdp", None),
            P("rep", "fsdp", None),
            P(),
        ),
        out_specs=(P("rep", "fsdp", None), P("rep", "fsdp", None)),
        check_vma=False,
    )
```

profile of v0, /device:TPU:0, one launch (start us, length us, event | category | flops | bytes accessed | tf_op | source)
XLA Modules:
  0.0 350.5 jit_solution(11786167551079003178)
XLA Ops:
  7.2 0.0 copy-start
  7.2 0.0 reduce-scatter.2.cloned.1.call-start
  7.2 1.5 copy-done
  8.8 9.3 %convolution_convert_fusion = bf16[4096,2048]{1,0:T(8,128)(2,1)} fusion(bf16[1,256,4096]{2,1,0:T(8,128)(2,1)S(1)} %copy-done, bf16[1,256,2048]{2,1,0:T(8,128)(2,1)} %param.9), kind=kOutput, calls=%fused_computation.2 | convolution fusion | flops 4303355904 | bytes 19922944 | tf_op jit(solution)/shard_map/dot_general | solution.py:20
  18.1 0.0 reduce-scatter.2.cloned.1.call-update
  18.1 8.6 %copy.17 = bf16[1,1024,2048]{2,0,1:T(2,128)(2,1)} copy(bf16[1,1024,2048]{2,1,0:T(8,128)(2,1)} %param.11) | data formatting | bytes 8388608 | tf_op args[3]
  26.7 0.6 broadcast.84
  27.3 26.8 %reduce = bf16[1024,2048]{1,0:T(8,128)(2,1)} reduce(bf16[1024,1,2048]{2,1,0:T(2,128)(2,1)} %bitcast.28, bf16[]{:T(256)} %broadcast.84), dimensions={1}, to_apply=%bitcast.26.reduce_sub_computation | reduce | bytes 8388610
  54.1 7.8 %reshape.105 = bf16[8,2,131072]{2,1,0:T(2,128)(2,1)} reshape(bf16[1024,2048]{1,0:T(8,128)(2,1)} %reduce) | data formatting | bytes 8388608
  61.9 5.2 %all-to-all-start = ((bf16[8,2,131072]{2,1,0:T(2,128)(2,1)}), bf16[8,2,131072]{2,1,0:T(2,128)(2,1)}, u32[]{:S(2)}, u32[]{:S(2)}) async-start(bf16[8,2,131072]{2,1,0:T(2,128)(2,1)} %reshape.105), calls=%async_computation | async-start | bytes 8388608 | tf_op jit(solution)/shard_map/all_to_all | solution.py:30
  67.1 8.6 %copy.16 = bf16[1,1024,2048]{2,0,1:T(2,128)(2,1)} copy(bf16[1,1024,2048]{2,1,0:T(8,128)(2,1)} %param.10) | data formatting | bytes 8388608 | tf_op args[2]
  75.7 26.8 %reduce.1 = bf16[1024,2048]{1,0:T(8,128)(2,1)} reduce(bf16[1024,1,2048]{2,1,0:T(2,128)(2,1)} %bitcast.29, bf16[]{:T(256)} %broadcast.84), dimensions={1}, to_apply=%bitcast.25.reduce_sub_computation | reduce | bytes 8388610
  102.5 7.8 %reshape.103 = bf16[8,2,131072]{2,1,0:T(2,128)(2,1)} reshape(bf16[1024,2048]{1,0:T(8,128)(2,1)} %reduce.1) | data formatting | bytes 8388608
  110.3 0.0 copy-start.2
  110.3 6.0 %all-to-all-done = bf16[8,2,131072]{2,1,0:T(2,128)(2,1)} async-done(((bf16[8,2,131072]{2,1,0:T(2,128)(2,1)}), bf16[8,2,131072]{2,1,0:T(2,128)(2,1)}, u32[]{:S(2)}, u32[]{:S(2)}) %all-to-all-start) | async-done | bytes 4194336 | tf_op jit(solution)/shard_map/all_to_all | solution.py:30
  116.3 4.7 %all-to-all-start.2 = ((bf16[8,2,131072]{2,1,0:T(2,128)(2,1)}), bf16[8,2,131072]{2,1,0:T(2,128)(2,1)}, u32[]{:S(2)}, u32[]{:S(2)}) async-start(bf16[8,2,131072]{2,1,0:T(2,128)(2,1)} %reshape.103), calls=%async_computation.2 | async-start | bytes 8388608 | tf_op jit(solution)/shard_map/all_to_all | solution.py:31
  121.0 0.0 copy-done.2
  121.1 8.8 %reshape.106 = bf16[1024,1,2048]{2,1,0:T(2,128)(2,1)} reshape(bf16[8,2,131072]{2,1,0:T(2,128)(2,1)} %all-to-all-done) | data formatting | bytes 8388608
  129.9 8.0 %copy.12 = bf16[1,1024,2048]{2,1,0:T(8,128)(2,1)} copy(bf16[1,1024,2048]{2,0,1:T(2,128)(2,1)} %bitcast.30) | data formatting | bytes 8388608
  137.9 32.1 %all-to-all-done.2 = bf16[8,2,131072]{2,1,0:T(2,128)(2,1)} async-done(((bf16[8,2,131072]{2,1,0:T(2,128)(2,1)}), bf16[8,2,131072]{2,1,0:T(2,128)(2,1)}, u32[]{:S(2)}, u32[]{:S(2)}) %all-to-all-start.2) | async-done | bytes 4194336 | tf_op jit(solution)/shard_map/all_to_all | solution.py:31
  170.0 8.8 %reshape.104 = bf16[1024,1,2048]{2,1,0:T(2,128)(2,1)} reshape(bf16[8,2,131072]{2,1,0:T(2,128)(2,1)} %all-to-all-done.2) | data formatting | bytes 8388608
  178.8 8.0 %copy.13 = bf16[1,1024,2048]{2,1,0:T(8,128)(2,1)} copy(bf16[1,1024,2048]{2,0,1:T(2,128)(2,1)} %bitcast.31) | data formatting | bytes 8388608
  186.8 5.0 %gather_fusion = bf16[8,128,2048]{2,1,0:T(8,128)(2,1)} fusion(bf16[8,128,2048]{2,1,0:T(8,128)(2,1)} %bitcast.32, s32[1024]{0:T(1024)S(1)} %pad_clamp_fusion), kind=kCustom, calls=%fused_computation.clone | custom fusion | bytes 8388640 | tf_op jit(solution)/shard_map/jit(_take)/gather | solution.py:33
  191.8 5.0 %gather_fusion.1 = bf16[8,128,2048]{2,1,0:T(8,128)(2,1)} fusion(bf16[8,128,2048]{2,1,0:T(8,128)(2,1)} %bitcast.33, s32[1024]{0:T(1024)S(1)} %pad_clamp_fusion), kind=kCustom, calls=%fused_computation.1.clone | custom fusion | bytes 8388640 | tf_op jit(solution)/shard_map/jit(_take)/gather | solution.py:34
  196.8 6.3 %broadcast_select_fusion.1 = (bf16[8,128,2048]{2,1,0:T(8,128)(2,1)}, bf16[8,128,2048]{2,1,0:T(8,128)(2,1)S(1)}) fusion(bf16[8,128,2048]{2,1,0:T(8,128)(2,1)} %gather_fusion, pred[8]{0:T(512)(128)(4,1)S(1)} %compare_and_fusion, bf16[8,128,2048]{2,1,0:T(8,128)(2,1)} %gather_fusion.1), kind=kLoop, calls=%fused_computation.16 | loop fusion | flops 4194304 | bytes 16777224 | tf_op jit(solution)/shard_map/jit(_take)/select_n | solution.py:33
  203.1 52.3 %all_to_all.42 = bf16[8,128,2048]{2,1,0:T(8,128)(2,1)} all-to-all(bf16[8,128,2048]{2,1,0:T(8,128)(2,1)S(1)} %get-tuple-element.6), channel_id=1, replica_groups=mesh['rep'=8,'fsdp'=4] {'rep'}, dimensions={0} | all-to-all | bytes 8388608 | tf_op jit(solution)/shard_map/all_to_all | solution.py:37
  255.5 4.8 %all-to-all-start.1 = ((bf16[8,128,2048]{2,1,0:T(8,128)(2,1)}), bf16[8,128,2048]{2,1,0:T(8,128)(2,1)}, u32[]{:S(2)}, u32[]{:S(2)}) async-start(bf16[8,128,2048]{2,1,0:T(8,128)(2,1)} %get-tuple-element.5), calls=%async_computation.1 | async-start | bytes 8388608 | tf_op jit(solution)/shard_map/all_to_all | solution.py:36
  260.2 41.0 %reduce-scatter.2.cloned.1.call-done = bf16[1024,2048]{1,0:T(8,128)(2,1)} async-done(((bf16[4096,2048]{1,0:T(8,128)(2,1)}), bf16[1024,2048]{1,0:T(8,128)(2,1)}) %reduce-scatter.2.cloned.1.call-update) | async-done | bytes 4194320 | tf_op jit(solution)/shard_map/reduce_scatter | solution.py:19
  301.3 4.9 %fusion.4 = f32[]{:T(128)} fusion(bf16[1024,2048]{1,0:T(8,128)(2,1)} %reduce-scatter.2.cloned.1.call-done), kind=kLoop, calls=%fused_computation.11 | loop fusion | flops 6291455 | bytes 4194308 | tf_op jit(solution)/shard_map/reduce_sum | solution.py:27
  306.2 2.9 all-to-all-done.1
  309.1 8.0 %multiply_convert_fusion = bf16[8,128,2048]{2,1,0:T(8,128)(2,1)} fusion(bf16[8,128,2048]{2,1,0:T(8,128)(2,1)} %all_to_all.42, bf16[8,128,2048]{2,1,0:T(8,128)(2,1)} %all-to-all-done.1), kind=kLoop, calls=%fused_computation.14 | loop fusion | flops 14680064 | bytes 12582912 | tf_op jit(solution)/shard_map/convert
  317.1 13.3 %psum.7 = f32[]{:T(128)} all-reduce(f32[]{:T(128)} %fusion.4), channel_id=1, replica_groups=mesh['rep'=8,'fsdp'=4] {'fsdp'}, use_global_device_ids=true, to_apply=%region_2.4 | all-reduce | flops 1 | bytes 8 | tf_op jit(solution)/shard_map/psum | solution.py:27
  331.2 0.0 copy-start.1
  331.2 12.5 %fusion.3 = (bf16[1,1024,2048]{2,1,0:T(8,128)(2,1)}, bf16[1,1024,2048]{2,1,0:T(8,128)(2,1)}) fusion(bf16[1,1024,2048]{2,1,0:T(8,128)(2,1)} %param.10, bf16[1024,2048]{1,0:T(8,128)(2,1)} %reduce-scatter.2.cloned.1.call-done, f32[]{:T(128)S(6)} %sqrt.3, bf16[1,1024,2048]{2,1,0:T(8,128)(2,1)} %param.11, bf16[1,1024,2048]{2,1,0:T(8,128)(2,1)} %param.12, ...), kind=kLoop, calls=%fused_computation.10 | loop fusion | flops 35651584 | bytes 29360132 | tf_op jit(solution)/shard_map/convert_element_type | solution.py:48
  343.7 0.0 copy-done.1
  (3 shorter events, 0.0 us)
Async XLA Ops:
  7.2 1.6 copy-start
  7.2 294.1 %reduce-scatter.2.cloned.1.call-start = ((), (), s32[]{:S(2)}) async-start(), calls=%async_computation.5 | async-start | bytes 20971520 | tf_op jit(solution)/shard_map/reduce_scatter | solution.py:19
  61.9 54.4 %all-to-all-start = ((bf16[8,2,131072]{2,1,0:T(2,128)(2,1)}), bf16[8,2,131072]{2,1,0:T(2,128)(2,1)}, u32[]{:S(2)}, u32[]{:S(2)}) async-start(bf16[8,2,131072]{2,1,0:T(2,128)(2,1)} %reshape.105), calls=%async_computation | async-start | bytes 8388608 | tf_op jit(solution)/shard_map/all_to_all | solution.py:30
  110.3 10.7 %copy-start.2 = (s32[8]{0:T(128)S(1)}, s32[8]{0:T(128)}, u32[]{:S(2)}) copy-start(s32[8]{0:T(128)} %param.13) | copy-start | bytes 100
  116.3 53.7 %all-to-all-start.2 = ((bf16[8,2,131072]{2,1,0:T(2,128)(2,1)}), bf16[8,2,131072]{2,1,0:T(2,128)(2,1)}, u32[]{:S(2)}, u32[]{:S(2)}) async-start(bf16[8,2,131072]{2,1,0:T(2,128)(2,1)} %reshape.103), calls=%async_computation.2 | async-start | bytes 8388608 | tf_op jit(solution)/shard_map/all_to_all | solution.py:31
  255.5 53.7 %all-to-all-start.1 = ((bf16[8,128,2048]{2,1,0:T(8,128)(2,1)}), bf16[8,128,2048]{2,1,0:T(8,128)(2,1)}, u32[]{:S(2)}, u32[]{:S(2)}) async-start(bf16[8,128,2048]{2,1,0:T(8,128)(2,1)} %get-tuple-element.5), calls=%async_computation.1 | async-start | bytes 8388608 | tf_op jit(solution)/shard_map/all_to_all | solution.py:36
  331.2 12.5 %copy-start.1 = (bf16[1,256,4096]{2,1,0:T(8,128)(2,1)S(1)}, bf16[1,256,4096]{2,1,0:T(8,128)(2,1)}, u32[]{:S(2)}) copy-start(bf16[1,256,4096]{2,1,0:T(8,128)(2,1)} %param.8) | copy-start | bytes 6291460
Sparse Core Ops, SparseCore 0:
  18.2 283.0 reduce-scatter.1
where the time goes:
time: 352 us; the launch traced here: 351 us
  other arithmetic  85.3 us (24%)
  waiting for transfers between devices  82 us (23%)
  local copies, waits for them, and re-layouts  78.6 us (22%)
  blocking collectives  65.6 us (19%)
  between operations  14.8 us (4%)
  starting transfers between devices  14.7 us (4%)
  matrix products  9.32 us (3%)
    unnamed x15, local copies, waits for them, and re-layouts  68.6 us
    unnamed x2, other arithmetic  53.6 us
    all_to_all x1, blocking collectives, on_device(): lax.all_to_all(mate_slow, 'rep', split_axis=0, concat_axis=1, tiled=True)  52.3 us
    reduce_scatter x1, waiting for transfers between devices, on_device(): lax.psum_scatter(lax.dot_general(local_x, local_g, (((0,), (0,)), ((), ()...  41 us
    all_to_all x1, waiting for transfers between devices, on_device(): lax.all_to_all(w_slow, 'rep', split_axis=1, concat_axis=0, tiled=True)  32.1 us
    psum x1, blocking collectives, on_device(): squares = lax.psum(jnp.sum(grad * grad), 'fsdp')  13.3 us
    convert_element_type x1, other arithmetic, on_device(): return (moment.astype(jnp.bfloat16), weights.astype(jnp.bfloat16))  12.5 us
    dot_general x1, matrix products, on_device(): lax.dot_general(local_x, local_g, (((0,), (0,)), ((), ())), preferred_ele...  9.32 us
  transfers between devices with their start and end apart: 4, of which 4 were waited for; matrix products, arithmetic and copies ran while one was open for 40% of the time, Pallas kernels for 0%

commit v1 on v0

v1 whole, which is shorter than its diff:
```python
import functools

import jax
import jax.numpy as jnp
from jax import lax
from jax.experimental import pallas as pl
from jax.experimental.pallas import tpu as pltpu
from jax.sharding import PartitionSpec as P

MESH = pl.DeviceIdType.MESH
CHUNKS = 4
F32 = jnp.float32
BF16 = jnp.bfloat16


def kernel(reps, n, *refs):
    C = CHUNKS
    (tok, cot, slow, drift, mom, partner, mom_out, w_out) = refs[:8]
    (wv, dv, mv, base, grad, tokv, cotv, mixsrc, mixin, squares, acc) = refs[8:19]
    owned = refs[19 : 19 + C]
    (ld, tsend, trecv, crecv, crsend, clsend, asend, arecv, bsend, brecv, qsend, qrecv, out_sem) = refs[19 + C :]
    me = lax.axis_index("rep")
    z = lax.axis_index("fsdp")
    rows = wv.shape[1]
    cw = wv.shape[2]
    rp = rows // reps
    cd = tokv.shape[2]

    def cols(c):
        return pl.ds(c * cw, cw)

    def load(kind, c):
        src, dst = ((slow, wv), (drift, dv), (mom, mv))[kind]
        return pltpu.make_async_copy(src.at[0, :, cols(c)], dst.at[c], ld.at[kind, c])

    def load_cot(q):
        return pltpu.make_async_copy(cot.at[0, :, cols(q)], cotv.at[q, z], ld.at[3, q])

    def tok_cols(k):
        return pl.ds(pl.multiple_of(k * cd, 128), cd)

    load_tok = pltpu.make_async_copy(tok.at[0, :, tok_cols(z)], tokv.at[z], ld.at[4, 0])

    for c in range(C):
        load(0, c).start()
        load(1, c).start()

    barrier = pltpu.get_barrier_semaphore()
    for d in range(1, n):
        pl.semaphore_signal(barrier, inc=1, device_id=(me, lax.rem(z + d, n)), device_id_type=MESH)

    def greet(d, _):
        pl.semaphore_signal(barrier, inc=1, device_id=(lax.rem(me + d, reps), z), device_id_type=MESH)
        return 0

    lax.fori_loop(1, reps, greet, 0)
    for q in range(C):
        load_cot(q).start()
    load_tok.start()
    for c in range(C):
        load(2, c).start()
    pl.semaphore_wait(barrier, reps - 1 + n - 1)

    def right_copy(q, s, src):
        return pltpu.make_async_remote_copy(
            src_ref=src, dst_ref=cotv.at[q, s], send_sem=crsend.at[q, s], recv_sem=crecv.at[q, s],
            device_id=(me, lax.min(z + 1, n - 1)), device_id_type=MESH)

    def left_copy(q, s, src):
        return pltpu.make_async_remote_copy(
            src_ref=src, dst_ref=cotv.at[q, s], send_sem=clsend.at[q, s], recv_sem=crecv.at[q, s],
            device_id=(me, lax.max(z - 1, 0)), device_id_type=MESH)

    for q in range(C):
        @pl.when(z + 1 < n)
        def _():
            right_copy(q, z, cot.at[0, :, cols(q)]).start()

        @pl.when(z > 0)
        def _():
            left_copy(q, z, cot.at[0, :, cols(q)]).start()

    def tok_copy(d):
        k = lax.rem(z + d, n)
        return pltpu.make_async_remote_copy(
            src_ref=tok.at[0, :, tok_cols(k)], dst_ref=tokv.at[z], send_sem=tsend.at[d], recv_sem=trecv.at[d],
            device_id=(me, k), device_id_type=MESH)

    for d in range(1, n):
        tok_copy(d).start()

    def first_leg(c, d):
        j = lax.rem(me + d, reps)
        return pltpu.make_async_remote_copy(
            src_ref=mixsrc.at[c, j], dst_ref=owned[c].at[me], send_sem=asend.at[c, d], recv_sem=arecv.at[c, d],
            device_id=(j, z), device_id_type=MESH)

    def first_leg_in(c, d):
        s = lax.rem(me + reps - d, reps)
        return pltpu.make_async_remote_copy(
            src_ref=mixsrc.at[c, s], dst_ref=owned[c].at[s], send_sem=asend.at[c, d], recv_sem=arecv.at[c, d],
            device_id=(s, z), device_id_type=MESH)

    def second_leg(c, d):
        j = lax.rem(me + d, reps)
        return pltpu.make_async_remote_copy(
            src_ref=mixsrc.at[c, j], dst_ref=mixin.at[c, me], send_sem=bsend.at[c, d], recv_sem=brecv.at[c, d],
            device_id=(j, z), device_id_type=MESH)

    def second_leg_in(c, d):
        s = lax.rem(me + reps - d, reps)
        return pltpu.make_async_remote_copy(
            src_ref=mixsrc.at[c, s], dst_ref=mixin.at[c, s], send_sem=bsend.at[c, d], recv_sem=brecv.at[c, d],
            device_id=(s, z), device_id_type=MESH)

    def block_rows(j):
        return pl.ds(pl.multiple_of(j * rp, rp), rp)

    def mix_block(c, j):
        part = block_rows(j)
        return (0.5 * (0.7 * dv[c, part, :].astype(F32) - 0.3 * wv[c, part, :].astype(F32))).astype(BF16)

    for c in range(C):
        load(0, c).wait()
        load(1, c).wait()

        def send_block(d, _):
            j = lax.rem(me + d, reps)
            mixsrc[c, j] = mix_block(c, j)
            first_leg(c, d).start()
            return 0

        lax.fori_loop(1, reps, send_block, 0)
        owned[c][me] = mix_block(c, me)

    def turn_round(c):
        def arrived(d, _):
            first_leg_in(c, d).wait_recv()
            first_leg(c, d).wait_send()
            return 0

        lax.fori_loop(1, reps, arrived, 0)

        def send_back(d, _):
            j = lax.rem(me + d, reps)
            mixsrc[c, j] = owned[c][partner[j]]
            second_leg(c, d).start()
            return 0

        lax.fori_loop(1, reps, send_back, 0)
        mixin[c, me] = owned[c][partner[me]]

    def finish_momentum(c):
        load(2, c).wait()

        def arrived(d, _):
            second_leg_in(c, d).wait_recv()
            return 0

        lax.fori_loop(1, reps, arrived, 0)

        def block(j, _):
            part = block_rows(j)
            own = wv[c, part, :].astype(F32)
            moment = (0.5 * mv[c, part, :].astype(F32) + 0.35 * dv[c, part, :].astype(F32) + 0.15 * own
                      + mixin[c, j].astype(F32))
            mv[c, part, :] = moment.astype(BF16)
            base[c, part, :] = own - moment
            return 0

        lax.fori_loop(0, reps, block, 0)
        pltpu.make_async_copy(mv.at[c], mom_out.at[0, :, cols(c)], out_sem.at[0, c]).start()

    tile = 256

    def product(q, s, first):
        def block(i, _):
            part = pl.ds(pl.multiple_of(i * tile, tile), tile)
            term = lax.dot_general(
                tokv[s, :, part], cotv[q, s], (((0,), (0,)), ((), ())), preferred_element_type=F32
            ).astype(BF16).astype(F32)
            if first:
                grad[q, part, :] = term
            else:
                grad[q, part, :] += term
            return 0

        lax.fori_loop(0, rows // tile, block, 0)

    def add_squares(q):
        def block(i, _):
            g = grad[q, pl.ds(pl.multiple_of(i * 64, 64), 64), :]
            acc[...] += jnp.sum((g * g).reshape(8, 8, cw), axis=0)
            return 0

        lax.fori_loop(0, rows // 64, block, 0)

    def arrive(h, q):
        @pl.when(z - h >= 0)
        def _():
            s = lax.max(z - h, 0)
            right_copy(q, s, cotv.at[q, s]).wait_recv()

            @pl.when(z + 1 < n)
            def _():
                right_copy(q, s, cotv.at[q, s]).start()

        @pl.when(z + h < n)
        def _():
            s = lax.min(z + h, n - 1)
            left_copy(q, s, cotv.at[q, s]).wait_recv()

            @pl.when(z > 0)
            def _():
                left_copy(q, s, cotv.at[q, s]).start()

    def multiply(h, q):
        @pl.when(z - h >= 0)
        def _():
            s = lax.max(z - h, 0)
            if q == 0:
                tok_in(s, h).wait_recv()
            product(q, s, False)

        @pl.when(z + h < n)
        def _():
            s = lax.min(z + h, n - 1)
            if q == 0:
                tok_in(s, n - h).wait_recv()
            product(q, s, False)

        @pl.when(lax.max(z, n - 1 - z) == h)
        def _():
            add_squares(q)

    def tok_in(s, d):
        return pltpu.make_async_remote_copy(
            src_ref=tokv.at[s], dst_ref=tokv.at[s], send_sem=tsend.at[d], recv_sem=trecv.at[d],
            device_id=(me, s), device_id_type=MESH)

    acc[...] = jnp.zeros_like(acc)
    load_tok.wait()
    for q in range(C):
        load_cot(q).wait()
        product(q, z, True)
    for h in range(1, n):
        for q in range(C):
            if h == n - 1:
                finish_momentum(q)
            arrive(h, q)
            if h == 1:
                turn_round(q)
            if h > 1:
                multiply(h - 1, q)
            if h == n - 1:
                multiply(h, q)

    part_sum = acc[:, 0:128]
    for k in range(1, cw // 128):
        part_sum = part_sum + acc[:, k * 128 : (k + 1) * 128]
    squares[z] = part_sum

    def squares_copy(d):
        k = lax.rem(z + d, n)
        return pltpu.make_async_remote_copy(
            src_ref=squares.at[z], dst_ref=squares.at[z], send_sem=qsend.at[d], recv_sem=qrecv.at[d],
            device_id=(me, k), device_id_type=MESH)

    for d in range(1, n):
        squares_copy(d).start()
    for d in range(1, n):
        s = lax.rem(z + n - d, n)
        pltpu.make_async_remote_copy(
            src_ref=squares.at[s], dst_ref=squares.at[s], send_sem=qsend.at[d], recv_sem=qrecv.at[d],
            device_id=(me, s), device_id_type=MESH).wait_recv()
    total = jnp.sum(jnp.sum(squares[...], axis=0), axis=(0, 1), keepdims=True)
    factor = 0.5 / jnp.sqrt(total / (rows * n * C * cw) + 1e-06)

    for q in range(C):
        def block(i, _):
            part = pl.ds(pl.multiple_of(i * 64, 64), 64)
            wv[q, part, :] = (base[q, part, :] - grad[q, part, :] * factor).astype(BF16)
            return 0

        lax.fori_loop(0, rows // 64, block, 0)
        pltpu.make_async_copy(wv.at[q], w_out.at[0, :, cols(q)], out_sem.at[1, q]).start()

    for d in range(1, n):
        tok_copy(d).wait_send()
        squares_copy(d).wait_send()
    for q in range(C):
        for h in range(0, n):
            @pl.when((z - h >= 0) & (z + 1 < n))
            def _():
                s = lax.max(z - h, 0)
                right_copy(q, s, cotv.at[q, s]).wait_send()

            @pl.when((z + h < n) & (z > 0))
            def _():
                s = lax.min(z + h, n - 1)
                left_copy(q, s, cotv.at[q, s]).wait_send()

        def sent(d, _):
            second_leg(q, d).wait_send()
            return 0

        lax.fori_loop(1, reps, sent, 0)
    for q in range(C):
        pltpu.make_async_copy(mv.at[q], mom_out.at[0, :, cols(q)], out_sem.at[0, q]).wait()
        pltpu.make_async_copy(wv.at[q], w_out.at[0, :, cols(q)], out_sem.at[1, q]).wait()


def on_device(reps, n, tokens, cotangent, w_slow, drift, momentum, partner):
    C = CHUNKS
    _, toks, d_in = tokens.shape
    _, rows, d_out = w_slow.shape
    cw, rp, cd = d_out // C, rows // reps, d_in // n
    hbm = pl.BlockSpec(memory_space=pl.ANY)
    dma = pltpu.SemaphoreType.DMA
    scratch = [
        pltpu.VMEM((C, rows, cw), BF16),
        pltpu.VMEM((C, rows, cw), BF16),
        pltpu.VMEM((C, rows, cw), BF16),
        pltpu.VMEM((C, rows, cw), F32),
        pltpu.VMEM((C, rows, cw), F32),
        pltpu.VMEM((n, toks, cd), BF16),
        pltpu.VMEM((C, n, toks, cw), BF16),
        pltpu.VMEM((C, reps, rp, cw), BF16),
        pltpu.VMEM((C, reps, rp, cw), BF16),
        pltpu.VMEM((n, 8, 128), F32),
        pltpu.VMEM((8, cw), F32),
    ]
    scratch += [pltpu.VMEM((reps, rp, cw), BF16) for _ in range(C)]
    scratch += [
        dma((5, C)), dma((n,)), dma((n,)), dma((C, n)), dma((C, n)), dma((C, n)),
        dma((C, reps)), dma((C, reps)), dma((C, reps)), dma((C, reps)), dma((n,)), dma((n,)), dma((2, C)),
    ]
    return pl.pallas_call(
        functools.partial(kernel, reps, n),
        out_shape=(jax.ShapeDtypeStruct(momentum.shape, BF16), jax.ShapeDtypeStruct(w_slow.shape, BF16)),
        in_specs=[hbm] * 5 + [pl.BlockSpec(memory_space=pltpu.SMEM)],
        out_specs=(hbm, hbm),
        scratch_shapes=scratch,
        compiler_params=pltpu.CompilerParams(
            collective_id=0, has_side_effects=True, vmem_limit_bytes=56 * 1024 * 1024
        ),
        cost_estimate=pl.CostEstimate(
            flops=2 * n * toks * rows * d_out, bytes_accessed=5 * rows * d_out * 2, transcendentals=0
        ),
    )(tokens, cotangent, w_slow, drift, momentum, partner)


def solution(mesh):
    spec = P("rep", "fsdp", None)
    return jax.shard_map(
        functools.partial(on_device, mesh.shape["rep"], mesh.shape["fsdp"]),
        mesh=mesh,
        in_specs=(spec, spec, spec, spec, spec, P()),
        out_specs=(spec, spec),
        check_vma=False,
    )
```

time: 352 us -> 127 us (0.36)
  Pallas kernels: 0 us -> 119 us
  other arithmetic: 85.3 us -> 0 us
  waiting for transfers between devices: 82 us -> 0 us
  local copies, waits for them, and re-layouts: 78.6 us -> 6.96 us
  blocking collectives: 65.6 us -> 0 us
  starting transfers between devices: 14.7 us -> 0 us
  between operations: 14.8 us -> 0.65 us
  matrix products: 9.32 us -> 0 us
    pallas_call x0 -> x1, Pallas kernels: none -> 119 us  [on_device(): pl.pallas_call(functools.partial(kernel, reps, n), out_shape=(jax.ShapeDt...]
    unnamed x15 -> x4, local copies, waits for them, and re-layouts: 68.6 us -> 6.96 us
    unnamed x2 -> x0, other arithmetic: 53.6 us -> none
    all_to_all x1 -> x0, blocking collectives: 52.3 us -> none  [on_device(): lax.all_to_all(mate_slow, 'rep', split_axis=0, concat_axis=1, tiled=True)]
    reduce_scatter x1 -> x0, waiting for transfers between devices: 41 us -> none  [on_device(): lax.psum_scatter(lax.dot_general(local_x, local_g, (((0,), (0,)), ((), ()...]
    all_to_all x3 -> x0, waiting for transfers between devices: 41 us -> none  [the longest x1 32.1 us: on_device(): lax.all_to_all(w_slow, 'rep', split_axis=1, concat_axis=0, tiled=True)]
    all_to_all x3 -> x0, starting transfers between devices: 14.7 us -> none  [the longest x1 5.2 us: on_device(): lax.all_to_all(drift, 'rep', split_axis=1, concat_axis=0, tiled=True)]
    psum x1 -> x0, blocking collectives: 13.3 us -> none  [on_device(): squares = lax.psum(jnp.sum(grad * grad), 'fsdp')]
  transfers between devices with their start and end apart: 4 -> 0, of which waited for: 4 -> 0; matrix products, arithmetic and copies ran while one was open for 40% -> 0% of each run, Pallas kernels for 0% -> 0%
where the time goes in v1:
time: 127 us
  Pallas kernels  119 us (94%)
  local copies, waits for them, and re-layouts  6.96 us (5%)
    pallas_call x1, Pallas kernels, on_device(): pl.pallas_call(functools.partial(kernel, reps, n), out_shape=(jax.ShapeDt...  119 us
    unnamed x4, local copies, waits for them, and re-layouts  6.96 us

profile of v1, /device:TPU:0, one launch (start us, length us, event | category | flops | bytes accessed | tf_op | source)
XLA Modules:
  0.0 127.0 jit_solution(17543927120406854888)
XLA Ops:
  0.6 119.4 %shard_map.77 = (bf16[1,1024,2048]{2,1,0:T(8,128)(2,1)}, bf16[1,1024,2048]{2,1,0:T(8,128)(2,1)}) custom-call(bf16[1,256,4096]{2,1,0:T(8,128)(2,1)} %refs_0_.1, bf16[1,256,2048]{2,1,0:T(8,128)(2,1)} %refs_1_.1, bf16[1,1024,2048]{2,1,0:T(8,128)(2,1)} %refs_2_.1, bf16[1,1024,2048]{2,1,0:T(8,128)(2,1)} %refs_3_.1, bf16[1,1024,2048]{2,1,0:T(8,128)(2,1)} %refs_4_.1, ...), custom_call_target="tpu_custom_call" | custom-call | flops 4294967296 | bytes 20971520 | tf_op jit(solution)/shard_map/pallas_call | solution.py:338
  120.0 0.0 copy-start
  120.0 4.9 %copy.10 = bf16[1,1024,2048]{2,1,0:T(8,128)(2,1)} copy(bf16[1,1024,2048]{2,1,0:T(8,128)(2,1)} %get-tuple-element.4) | data formatting | bytes 8388608
  125.0 0.0 copy-done
  125.0 2.0 %copy.11 = bf16[1,1024,2048]{2,1,0:T(8,128)(2,1)} copy(bf16[1,1024,2048]{2,1,0:T(8,128)(2,1)S(1)} %copy-done) | data formatting | bytes 8388608
Async XLA Ops:
  120.0 5.0 %copy-start = (bf16[1,1024,2048]{2,1,0:T(8,128)(2,1)S(1)}, bf16[1,1024,2048]{2,1,0:T(8,128)(2,1)}, u32[]{:S(2)}) copy-start(bf16[1,1024,2048]{2,1,0:T(8,128)(2,1)} %get-tuple-element.5) | copy-start | bytes 12582916

commit v2 on v1

--- a/solution.py
+++ b/solution.py
@@ -15,10 +15,10 @@
 
 def kernel(reps, n, *refs):
     C = CHUNKS
-    (tok, cot, slow, drift, mom, partner, mom_out, w_out) = refs[:8]
-    (wv, dv, mv, base, grad, tokv, cotv, mixsrc, mixin, squares, acc) = refs[8:19]
+    (tok, cot, slow, drift, mom, partner, mom_out, base, grad, factor_out) = refs[:10]
+    (wv, dv, mv, tokv, cotv, mixsrc, mixin, squares, acc) = refs[10:19]
     owned = refs[19 : 19 + C]
-    (ld, tsend, trecv, crecv, crsend, clsend, asend, arecv, bsend, brecv, qsend, qrecv, out_sem) = refs[19 + C :]
+    (ld, tsend, trecv, crecv, crsend, clsend, asend, arecv, bsend, brecv, qsend, qrecv) = refs[19 + C :]
     me = lax.axis_index("rep")
     z = lax.axis_index("fsdp")
     rows = wv.shape[1]
@@ -164,12 +164,11 @@
             own = wv[c, part, :].astype(F32)
             moment = (0.5 * mv[c, part, :].astype(F32) + 0.35 * dv[c, part, :].astype(F32) + 0.15 * own
                       + mixin[c, j].astype(F32))
-            mv[c, part, :] = moment.astype(BF16)
-            base[c, part, :] = own - moment
+            mom_out[0, part, cols(c)] = moment.astype(BF16)
+            base[0, part, cols(c)] = own - moment
             return 0
 
         lax.fori_loop(0, reps, block, 0)
-        pltpu.make_async_copy(mv.at[c], mom_out.at[0, :, cols(c)], out_sem.at[0, c]).start()
 
     tile = 256
 
@@ -180,16 +179,16 @@
                 tokv[s, :, part], cotv[q, s], (((0,), (0,)), ((), ())), preferred_element_type=F32
             ).astype(BF16).astype(F32)
             if first:
-                grad[q, part, :] = term
+                grad[0, part, cols(q)] = term
             else:
-                grad[q, part, :] += term
+                grad[0, part, cols(q)] += term
             return 0
 
         lax.fori_loop(0, rows // tile, block, 0)
 
     def add_squares(q):
         def block(i, _):
-            g = grad[q, pl.ds(pl.multiple_of(i * 64, 64), 64), :]
+            g = grad[0, pl.ds(pl.multiple_of(i * 64, 64), 64), cols(q)]
             acc[...] += jnp.sum((g * g).reshape(8, 8, cw), axis=0)
             return 0
 
@@ -275,15 +274,7 @@
             device_id=(me, s), device_id_type=MESH).wait_recv()
     total = jnp.sum(jnp.sum(squares[...], axis=0), axis=(0, 1), keepdims=True)
     factor = 0.5 / jnp.sqrt(total / (rows * n * C * cw) + 1e-06)
-
-    for q in range(C):
-        def block(i, _):
-            part = pl.ds(pl.multiple_of(i * 64, 64), 64)
-            wv[q, part, :] = (base[q, part, :] - grad[q, part, :] * factor).astype(BF16)
-            return 0
-
-        lax.fori_loop(0, rows // 64, block, 0)
-        pltpu.make_async_copy(wv.at[q], w_out.at[0, :, cols(q)], out_sem.at[1, q]).start()
+    factor_out[...] = jnp.broadcast_to(factor[None], factor_out.shape)
 
     for d in range(1, n):
         tok_copy(d).wait_send()
@@ -305,9 +296,6 @@
             return 0
 
         lax.fori_loop(1, reps, sent, 0)
-    for q in range(C):
-        pltpu.make_async_copy(mv.at[q], mom_out.at[0, :, cols(q)], out_sem.at[0, q]).wait()
-        pltpu.make_async_copy(wv.at[q], w_out.at[0, :, cols(q)], out_sem.at[1, q]).wait()
 
 
 def on_device(reps, n, tokens, cotangent, w_slow, drift, momentum, partner):
@@ -321,8 +309,6 @@
         pltpu.VMEM((C, rows, cw), BF16),
         pltpu.VMEM((C, rows, cw), BF16),
         pltpu.VMEM((C, rows, cw), BF16),
-        pltpu.VMEM((C, rows, cw), F32),
-        pltpu.VMEM((C, rows, cw), F32),
         pltpu.VMEM((n, toks, cd), BF16),
         pltpu.VMEM((C, n, toks, cw), BF16),
         pltpu.VMEM((C, reps, rp, cw), BF16),
@@ -333,21 +319,27 @@
     scratch += [pltpu.VMEM((reps, rp, cw), BF16) for _ in range(C)]
     scratch += [
         dma((5, C)), dma((n,)), dma((n,)), dma((C, n)), dma((C, n)), dma((C, n)),
-        dma((C, reps)), dma((C, reps)), dma((C, reps)), dma((C, reps)), dma((n,)), dma((n,)), dma((2, C)),
+        dma((C, reps)), dma((C, reps)), dma((C, reps)), dma((C, reps)), dma((n,)), dma((n,)),
     ]
-    return pl.pallas_call(
+    moment, base, grad, factor = pl.pallas_call(
         functools.partial(kernel, reps, n),
-        out_shape=(jax.ShapeDtypeStruct(momentum.shape, BF16), jax.ShapeDtypeStruct(w_slow.shape, BF16)),
+        out_shape=(
+            pltpu.VMEM(momentum.shape, BF16),
+            pltpu.VMEM(w_slow.shape, F32),
+            pltpu.VMEM(w_slow.shape, F32),
+            pltpu.VMEM((1, 1, d_out), F32),
+        ),
         in_specs=[hbm] * 5 + [pl.BlockSpec(memory_space=pltpu.SMEM)],
-        out_specs=(hbm, hbm),
+        out_specs=[pl.BlockSpec(memory_space=pltpu.VMEM)] * 4,
         scratch_shapes=scratch,
         compiler_params=pltpu.CompilerParams(
-            collective_id=0, has_side_effects=True, vmem_limit_bytes=56 * 1024 * 1024
+            collective_id=0, has_side_effects=True, vmem_limit_bytes=34 * 1024 * 1024
         ),
         cost_estimate=pl.CostEstimate(
             flops=2 * n * toks * rows * d_out, bytes_accessed=5 * rows * d_out * 2, transcendentals=0
         ),
     )(tokens, cotangent, w_slow, drift, momentum, partner)
+    return moment, (base - grad * factor).astype(BF16)
 
 
 def solution(mesh):

time: 127 us -> 137 us (1.079)
  other arithmetic: 0 us -> 10.2 us
  Pallas kernels: 119 us -> 117 us
  local copies, waits for them, and re-layouts: 6.96 us -> 8.46 us
    convert_element_type x0 -> x1, other arithmetic: none -> 10.2 us  [on_device(): return (moment, (base - grad * factor).astype(BF16))]
    pallas_call x1, Pallas kernels: 119 us -> 117 us  [on_device(): pl.pallas_call(functools.partial(kernel, reps, n), out_shape=(pltpu.VMEM(...]
    unnamed x4 -> x5, local copies, waits for them, and re-layouts: 6.96 us -> 8.46 us
where the time goes in v2:
time: 137 us
  Pallas kernels  117 us (85%)
  other arithmetic  10.2 us (7%)
  local copies, waits for them, and re-layouts  8.46 us (6%)
    pallas_call x1, Pallas kernels, on_device(): pl.pallas_call(functools.partial(kernel, reps, n), out_shape=(pltpu.VMEM(...  117 us
    convert_element_type x1, other arithmetic, on_device(): return (moment, (base - grad * factor).astype(BF16))  10.2 us
    unnamed x5, local copies, waits for them, and re-layouts  8.46 us

profile of v2, /device:TPU:0, one launch (start us, length us, event | category | flops | bytes accessed | tf_op | source)
XLA Modules:
  0.0 136.6 jit_solution(1824486000664904305)
XLA Ops:
  0.6 117.3 %shard_map.77 = (bf16[1,1024,2048]{2,1,0:T(8,128)(2,1)S(1)}, f32[1,1024,2048]{2,1,0:T(8,128)S(1)}, f32[1,1024,2048]{2,1,0:T(8,128)S(1)}, f32[1,1,2048]{2,1,0:T(1,128)S(1)}) custom-call(bf16[1,256,4096]{2,1,0:T(8,128)(2,1)} %refs_0_.1, bf16[1,256,2048]{2,1,0:T(8,128)(2,1)} %refs_1_.1, bf16[1,1024,2048]{2,1,0:T(8,128)(2,1)} %refs_2_.1, ...), custom_call_target="tpu_custom_call" | custom-call | flops 4294967296 | bytes 20971520 | tf_op jit(solution)/shard_map/pallas_call | solution.py:324
  117.9 0.0 copy-start
  117.9 3.2 %copy-done = f32[1,1024,2048]{2,1,0:T(8,128)} copy-done((f32[1,1024,2048]{2,1,0:T(8,128)}, f32[1,1024,2048]{2,1,0:T(8,128)S(1)}, u32[]{:S(2)}) %copy-start) | copy-done | bytes 8388632
  121.2 0.0 copy-start.1
  121.2 3.2 %copy-done.1 = f32[1,1024,2048]{2,1,0:T(8,128)} copy-done((f32[1,1024,2048]{2,1,0:T(8,128)}, f32[1,1024,2048]{2,1,0:T(8,128)S(1)}, u32[]{:S(2)}) %copy-start.1) | copy-done | bytes 8388632
  124.4 2.0 %copy.9 = bf16[1,1024,2048]{2,1,0:T(8,128)(2,1)} copy(bf16[1,1024,2048]{2,1,0:T(8,128)(2,1)S(1)} %get-tuple-element.10) | data formatting | bytes 8388608
  126.4 10.2 %subtract_convert_fusion = bf16[1,1024,2048]{2,1,0:T(8,128)(2,1)} fusion(f32[1,1024,2048]{2,1,0:T(8,128)} %copy-done, f32[1,1024,2048]{2,1,0:T(8,128)} %copy-done.1, f32[2048]{0:T(1024)S(1)} %bitcast.1), kind=kLoop, calls=%fused_computation | loop fusion | flops 6291456 | bytes 20979712 | tf_op jit(solution)/shard_map/convert_element_type | solution.py:342
Async XLA Ops:
  117.9 3.2 %copy-start = (f32[1,1024,2048]{2,1,0:T(8,128)}, f32[1,1024,2048]{2,1,0:T(8,128)S(1)}, u32[]{:S(2)}) copy-start(f32[1,1024,2048]{2,1,0:T(8,128)S(1)} %get-tuple-element.7) | copy-start | bytes 25165828
  121.2 3.2 %copy-start.1 = (f32[1,1024,2048]{2,1,0:T(8,128)}, f32[1,1024,2048]{2,1,0:T(8,128)S(1)}, u32[]{:S(2)}) copy-start(f32[1,1024,2048]{2,1,0:T(8,128)S(1)} %get-tuple-element.8) | copy-start | bytes 25165828

commit v3 on v2

--- a/solution.py
+++ b/solution.py
@@ -16,9 +16,9 @@
 def kernel(reps, n, *refs):
     C = CHUNKS
     (tok, cot, slow, drift, mom, partner, mom_out, base, grad, factor_out) = refs[:10]
-    (wv, dv, mv, tokv, cotv, mixsrc, mixin, squares, acc) = refs[10:19]
-    owned = refs[19 : 19 + C]
-    (ld, tsend, trecv, crecv, crsend, clsend, asend, arecv, bsend, brecv, qsend, qrecv) = refs[19 + C :]
+    (wv, dv, mv, tokv, cotv, mixsrc, mixin, squares, acc, tokt) = refs[10:20]
+    owned = refs[20 : 20 + C]
+    (ld, tsend, trecv, crecv, crsend, clsend, asend, arecv, bsend, brecv, qsend, qrecv) = refs[20 + C :]
     me = lax.axis_index("rep")
     z = lax.axis_index("fsdp")
     rows = wv.shape[1]
@@ -172,12 +172,18 @@
 
     tile = 256
 
+    def turn_tokens(s):
+        def block(i, _):
+            part = pl.ds(pl.multiple_of(i * tile, tile), tile)
+            tokt[s, part, :] = tokv[s, :, part].T
+            return 0
+
+        lax.fori_loop(0, rows // tile, block, 0)
+
     def product(q, s, first):
         def block(i, _):
             part = pl.ds(pl.multiple_of(i * tile, tile), tile)
-            term = lax.dot_general(
-                tokv[s, :, part], cotv[q, s], (((0,), (0,)), ((), ())), preferred_element_type=F32
-            ).astype(BF16).astype(F32)
+            term = jnp.dot(tokt[s, part, :], cotv[q, s], preferred_element_type=F32).astype(BF16).astype(F32)
             if first:
                 grad[0, part, cols(q)] = term
             else:
@@ -219,6 +225,7 @@
             s = lax.max(z - h, 0)
             if q == 0:
                 tok_in(s, h).wait_recv()
+                turn_tokens(s)
             product(q, s, False)
 
         @pl.when(z + h < n)
@@ -226,6 +233,7 @@
             s = lax.min(z + h, n - 1)
             if q == 0:
                 tok_in(s, n - h).wait_recv()
+                turn_tokens(s)
             product(q, s, False)
 
         @pl.when(lax.max(z, n - 1 - z) == h)
@@ -239,13 +247,17 @@
 
     acc[...] = jnp.zeros_like(acc)
     load_tok.wait()
+    turn_tokens(z)
     for q in range(C):
         load_cot(q).wait()
         product(q, z, True)
     for h in range(1, n):
         for q in range(C):
-            if h == n - 1:
-                finish_momentum(q)
+            if h == n - 1 and q == C - 2:
+                for c in range(C - 2):
+                    finish_momentum(c)
+            if h == n - 1 and q == C - 1:
+                finish_momentum(C - 2)
             arrive(h, q)
             if h == 1:
                 turn_round(q)
@@ -267,6 +279,7 @@
 
     for d in range(1, n):
         squares_copy(d).start()
+    finish_momentum(C - 1)
     for d in range(1, n):
         s = lax.rem(z + n - d, n)
         pltpu.make_async_remote_copy(
@@ -296,6 +309,28 @@
             return 0
 
         lax.fori_loop(1, reps, sent, 0)
+
+
+def last_pass(parts, moment, base, grad, factor, mom_out, w_out, held, sem):
+    depth = held.shape[1]
+    step = 16
+    mom_copy = pltpu.make_async_copy(moment, mom_out, sem.at[parts])
+    mom_copy.start()
+    copies = []
+    for k in range(parts):
+        def block(i, _):
+            part = pl.ds(pl.multiple_of(k * depth + i * step, step), step)
+            held[k, pl.ds(pl.multiple_of(i * step, step), step), :] = (
+                base[0, part, :] - grad[0, part, :] * factor[0]
+            ).astype(BF16)
+            return 0
+
+        lax.fori_loop(0, depth // step, block, 0)
+        copies.append(pltpu.make_async_copy(held.at[k], w_out.at[0, pl.ds(k * depth, depth), :], sem.at[k]))
+        copies[-1].start()
+    for copy in copies:
+        copy.wait()
+    mom_copy.wait()
 
 
 def on_device(reps, n, tokens, cotangent, w_slow, drift, momentum, partner):
@@ -315,6 +350,7 @@
         pltpu.VMEM((C, reps, rp, cw), BF16),
         pltpu.VMEM((n, 8, 128), F32),
         pltpu.VMEM((8, cw), F32),
+        pltpu.VMEM((n, cd, toks), BF16),
     ]
     scratch += [pltpu.VMEM((reps, rp, cw), BF16) for _ in range(C)]
     scratch += [
@@ -339,7 +375,16 @@
             flops=2 * n * toks * rows * d_out, bytes_accessed=5 * rows * d_out * 2, transcendentals=0
         ),
     )(tokens, cotangent, w_slow, drift, momentum, partner)
-    return moment, (base - grad * factor).astype(BF16)
+    parts = 8
+    return pl.pallas_call(
+        functools.partial(last_pass, parts),
+        out_shape=(jax.ShapeDtypeStruct(momentum.shape, BF16), jax.ShapeDtypeStruct(w_slow.shape, BF16)),
+        in_specs=[pl.BlockSpec(memory_space=pltpu.VMEM)] * 4,
+        out_specs=(hbm, hbm),
+        scratch_shapes=[pltpu.VMEM((parts, rows // parts, d_out), BF16), dma((parts + 1,))],
+        compiler_params=pltpu.CompilerParams(vmem_limit_bytes=8 * 1024 * 1024),
+        cost_estimate=pl.CostEstimate(flops=2 * rows * d_out, bytes_accessed=4 * rows * d_out, transcendentals=0),
+    )(moment, base, grad, factor)
 
 
 def solution(mesh):

time: 137 us -> 121 us (0.88)
  other arithmetic: 10.2 us -> 0 us
  local copies, waits for them, and re-layouts: 8.46 us -> 0 us
  Pallas kernels: 117 us -> 120 us
    convert_element_type x1 -> x0, other arithmetic: 10.2 us -> none  [on_device(): return (moment, (base - grad * factor).astype(BF16))]
    unnamed x5 -> x0, local copies, waits for them, and re-layouts: 8.46 us -> none
    pallas_call x0 -> x1, Pallas kernels: none -> 3.36 us  [on_device(): pl.pallas_call(functools.partial(last_pass, parts), out_shape=(jax.ShapeD...]
where the time goes in v3:
time: 121 us
  Pallas kernels  120 us (99%)
    pallas_call x1, Pallas kernels, on_device(): pl.pallas_call(functools.partial(kernel, reps, n), out_shape=(pltpu.VMEM(...  117 us
    pallas_call x1, Pallas kernels, on_device(): pl.pallas_call(functools.partial(last_pass, parts), out_shape=(jax.ShapeD...  3.36 us

profile of v3, /device:TPU:0, one launch (start us, length us, event | category | flops | bytes accessed | tf_op | source)
XLA Modules:
  0.0 121.1 jit_solution(17640635475754887537)
XLA Ops:
  0.6 117.1 %shard_map.77 = (bf16[1,1024,2048]{2,1,0:T(8,128)(2,1)S(1)}, f32[1,1024,2048]{2,1,0:T(8,128)S(1)}, f32[1,1024,2048]{2,1,0:T(8,128)S(1)}, f32[1,1,2048]{2,1,0:T(1,128)S(1)}) custom-call(bf16[1,256,4096]{2,1,0:T(8,128)(2,1)} %refs_0_.1, bf16[1,256,2048]{2,1,0:T(8,128)(2,1)} %refs_1_.1, bf16[1,1024,2048]{2,1,0:T(8,128)(2,1)} %refs_2_.1, ...), custom_call_target="tpu_custom_call" | custom-call | flops 4294967296 | bytes 20971520 | tf_op jit(solution)/shard_map/pallas_call | solution.py:360
  117.7 3.4 %shard_map.78 = (bf16[1,1024,2048]{2,1,0:T(8,128)(2,1)}, bf16[1,1024,2048]{2,1,0:T(8,128)(2,1)}) custom-call(bf16[1,1024,2048]{2,1,0:T(8,128)(2,1)S(1)} %get-tuple-element.6.moment, f32[1,1024,2048]{2,1,0:T(8,128)S(1)} %get-tuple-element.7.base, f32[1,1024,2048]{2,1,0:T(8,128)S(1)} %get-tuple-element.8.grad, f32[1,1,2048]{2,1,0:T(1,128)S(1)} %get-tuple-element.9.factor), custom_call_target="tpu_custom_call" | custom-call | flops 4194304 | bytes 8388608 | tf_op jit(solution)/shard_map/pallas_call | solution.py:379

commit v4 on v3

--- a/solution.py
+++ b/solution.py
@@ -26,6 +26,26 @@
     rp = rows // reps
     cd = tokv.shape[2]
 
+    bits = reps.bit_length() - 1
+    paired = reps == 1 << bits
+
+    def bit(value, i):
+        return lax.rem(lax.div(value, 1 << i), 2)
+
+    def to(d):
+        if not paired:
+            return lax.rem(me + d, reps)
+        return sum((bit(me, i) + bit(d, i) - 2 * bit(me, i) * bit(d, i)) * (1 << i) for i in range(bits))
+
+    def source(d):
+        return to(d) if paired else lax.rem(me + reps - d, reps)
+
+    def distance(k):
+        if not paired or bits < 3:
+            return k
+        d = lax.rem(k, reps - 1) + 1
+        return d + 2 * (bit(d, 1) - bit(d, 2)) * lax.rem(me, 2)
+
     def cols(c):
         return pl.ds(c * cw, cw)
 
@@ -90,25 +110,25 @@
         tok_copy(d).start()
 
     def first_leg(c, d):
-        j = lax.rem(me + d, reps)
+        j = to(d)
         return pltpu.make_async_remote_copy(
             src_ref=mixsrc.at[c, j], dst_ref=owned[c].at[me], send_sem=asend.at[c, d], recv_sem=arecv.at[c, d],
             device_id=(j, z), device_id_type=MESH)
 
     def first_leg_in(c, d):
-        s = lax.rem(me + reps - d, reps)
+        s = source(d)
         return pltpu.make_async_remote_copy(
             src_ref=mixsrc.at[c, s], dst_ref=owned[c].at[s], send_sem=asend.at[c, d], recv_sem=arecv.at[c, d],
             device_id=(s, z), device_id_type=MESH)
 
     def second_leg(c, d):
-        j = lax.rem(me + d, reps)
+        j = to(d)
         return pltpu.make_async_remote_copy(
             src_ref=mixsrc.at[c, j], dst_ref=mixin.at[c, me], send_sem=bsend.at[c, d], recv_sem=brecv.at[c, d],
             device_id=(j, z), device_id_type=MESH)
 
     def second_leg_in(c, d):
-        s = lax.rem(me + reps - d, reps)
+        s = source(d)
         return pltpu.make_async_remote_copy(
             src_ref=mixsrc.at[c, s], dst_ref=mixin.at[c, s], send_sem=bsend.at[c, d], recv_sem=brecv.at[c, d],
             device_id=(s, z), device_id_type=MESH)
@@ -124,8 +144,9 @@
         load(0, c).wait()
         load(1, c).wait()
 
-        def send_block(d, _):
-            j = lax.rem(me + d, reps)
+        def send_block(k, _):
+            d = distance(k)
+            j = to(d)
             mixsrc[c, j] = mix_block(c, j)
             first_leg(c, d).start()
             return 0
@@ -141,8 +162,9 @@
 
         lax.fori_loop(1, reps, arrived, 0)
 
-        def send_back(d, _):
-            j = lax.rem(me + d, reps)
+        def send_back(k, _):
+            d = distance(k)
+            j = to(d)
             mixsrc[c, j] = owned[c][partner[j]]
             second_leg(c, d).start()
             return 0

time: 121 us -> 121 us (level)
  no operation moved by 1% of the time
where the time goes in v4:
time: 121 us
  Pallas kernels  120 us (99%)
    pallas_call x1, Pallas kernels, on_device(): pl.pallas_call(functools.partial(kernel, reps, n), out_shape=(pltpu.VMEM(...  117 us
    pallas_call x1, Pallas kernels, on_device(): pl.pallas_call(functools.partial(last_pass, parts), out_shape=(jax.ShapeD...  3.36 us

profile of v4, /device:TPU:0, one launch (start us, length us, event | category | flops | bytes accessed | tf_op | source)
XLA Modules:
  0.0 121.1 jit_solution(10393312777366943003)
XLA Ops:
  0.6 117.1 %shard_map.77 = (bf16[1,1024,2048]{2,1,0:T(8,128)(2,1)S(1)}, f32[1,1024,2048]{2,1,0:T(8,128)S(1)}, f32[1,1024,2048]{2,1,0:T(8,128)S(1)}, f32[1,1,2048]{2,1,0:T(1,128)S(1)}) custom-call(bf16[1,256,4096]{2,1,0:T(8,128)(2,1)} %refs_0_.1, bf16[1,256,2048]{2,1,0:T(8,128)(2,1)} %refs_1_.1, bf16[1,1024,2048]{2,1,0:T(8,128)(2,1)} %refs_2_.1, ...), custom_call_target="tpu_custom_call" | custom-call | flops 4294967296 | bytes 20971520 | tf_op jit(solution)/shard_map/pallas_call | solution.py:382
  117.7 3.4 %shard_map.78 = (bf16[1,1024,2048]{2,1,0:T(8,128)(2,1)}, bf16[1,1024,2048]{2,1,0:T(8,128)(2,1)}) custom-call(bf16[1,1024,2048]{2,1,0:T(8,128)(2,1)S(1)} %get-tuple-element.6.moment, f32[1,1024,2048]{2,1,0:T(8,128)S(1)} %get-tuple-element.7.base, f32[1,1024,2048]{2,1,0:T(8,128)S(1)} %get-tuple-element.8.grad, f32[1,1,2048]{2,1,0:T(1,128)S(1)} %get-tuple-element.9.factor), custom_call_target="tpu_custom_call" | custom-call | flops 4194304 | bytes 8388608 | tf_op jit(solution)/shard_map/pallas_call | solution.py:401

commit v5 on v4

--- a/solution.py
+++ b/solution.py
@@ -106,9 +106,6 @@
             src_ref=tok.at[0, :, tok_cols(k)], dst_ref=tokv.at[z], send_sem=tsend.at[d], recv_sem=trecv.at[d],
             device_id=(me, k), device_id_type=MESH)
 
-    for d in range(1, n):
-        tok_copy(d).start()
-
     def first_leg(c, d):
         j = to(d)
         return pltpu.make_async_remote_copy(
@@ -140,7 +137,7 @@
         part = block_rows(j)
         return (0.5 * (0.7 * dv[c, part, :].astype(F32) - 0.3 * wv[c, part, :].astype(F32))).astype(BF16)
 
-    for c in range(C):
+    def send_mix(c):
         load(0, c).wait()
         load(1, c).wait()
 
@@ -267,26 +264,39 @@
             src_ref=tokv.at[s], dst_ref=tokv.at[s], send_sem=tsend.at[d], recv_sem=trecv.at[d],
             device_id=(me, s), device_id_type=MESH)
 
+    send_mix(0)
+    send_mix(1)
     acc[...] = jnp.zeros_like(acc)
     load_tok.wait()
     turn_tokens(z)
     for q in range(C):
+        arrive(1, q)
+        if q % 2 == 1 and 2 + q // 2 < C:
+            send_mix(2 + q // 2)
+    for d in range(1, n):
+        tok_copy(d).start()
+    turn_round(0)
+    for q in range(C):
         load_cot(q).wait()
         product(q, z, True)
-    for h in range(1, n):
+        if n > 3:
+            arrive(2, q)
+        if q + 1 < C:
+            turn_round(q + 1)
+    for h in range(3, n - 1):
         for q in range(C):
-            if h == n - 1 and q == C - 2:
-                for c in range(C - 2):
-                    finish_momentum(c)
-            if h == n - 1 and q == C - 1:
-                finish_momentum(C - 2)
             arrive(h, q)
-            if h == 1:
-                turn_round(q)
-            if h > 1:
-                multiply(h - 1, q)
-            if h == n - 1:
-                multiply(h, q)
+    for h in range(1, n - 1):
+        for q in range(C):
+            multiply(h, q)
+    for q in range(C):
+        if q == C - 2:
+            for c in range(C - 2):
+                finish_momentum(c)
+        if q == C - 1:
+            finish_momentum(C - 2)
+        arrive(n - 1, q)
+        multiply(n - 1, q)
 
     part_sum = acc[:, 0:128]
     for k in range(1, cw // 128):

time: 121 us -> 122 us (level)
  no operation moved by 1% of the time
where the time goes in v5:
time: 122 us
  Pallas kernels  121 us (99%)
    pallas_call x1, Pallas kernels, on_device(): pl.pallas_call(functools.partial(kernel, reps, n), out_shape=(pltpu.VMEM(...  118 us
    pallas_call x1, Pallas kernels, on_device(): pl.pallas_call(functools.partial(last_pass, parts), out_shape=(jax.ShapeD...  3.36 us

profile of v5, /device:TPU:0, one launch (start us, length us, event | category | flops | bytes accessed | tf_op | source)
XLA Modules:
  0.0 121.7 jit_solution(7478795570021531105)
XLA Ops:
  0.6 117.7 %shard_map.77 = (bf16[1,1024,2048]{2,1,0:T(8,128)(2,1)S(1)}, f32[1,1024,2048]{2,1,0:T(8,128)S(1)}, f32[1,1024,2048]{2,1,0:T(8,128)S(1)}, f32[1,1,2048]{2,1,0:T(1,128)S(1)}) custom-call(bf16[1,256,4096]{2,1,0:T(8,128)(2,1)} %refs_0_.1, bf16[1,256,2048]{2,1,0:T(8,128)(2,1)} %refs_1_.1, bf16[1,1024,2048]{2,1,0:T(8,128)(2,1)} %refs_2_.1, ...), custom_call_target="tpu_custom_call" | custom-call | flops 4294967296 | bytes 20971520 | tf_op jit(solution)/shard_map/pallas_call | solution.py:392
  118.3 3.4 %shard_map.78 = (bf16[1,1024,2048]{2,1,0:T(8,128)(2,1)}, bf16[1,1024,2048]{2,1,0:T(8,128)(2,1)}) custom-call(bf16[1,1024,2048]{2,1,0:T(8,128)(2,1)S(1)} %get-tuple-element.6.moment, f32[1,1024,2048]{2,1,0:T(8,128)S(1)} %get-tuple-element.7.base, f32[1,1024,2048]{2,1,0:T(8,128)S(1)} %get-tuple-element.8.grad, f32[1,1,2048]{2,1,0:T(1,128)S(1)} %get-tuple-element.9.factor), custom_call_target="tpu_custom_call" | custom-call | flops 4194304 | bytes 8388608 | tf_op jit(solution)/shard_map/pallas_call | solution.py:411

commit v6 on v4

--- a/solution.py
+++ b/solution.py
@@ -91,6 +91,15 @@
             src_ref=src, dst_ref=cotv.at[q, s], send_sem=clsend.at[q, s], recv_sem=crecv.at[q, s],
             device_id=(me, lax.max(z - 1, 0)), device_id_type=MESH)
 
+    def tok_copy(d):
+        k = lax.rem(z + d, n)
+        return pltpu.make_async_remote_copy(
+            src_ref=tok.at[0, :, tok_cols(k)], dst_ref=tokv.at[z], send_sem=tsend.at[d], recv_sem=trecv.at[d],
+            device_id=(me, k), device_id_type=MESH)
+
+    for d in range(1, n):
+        tok_copy(d).start()
+
     for q in range(C):
         @pl.when(z + 1 < n)
         def _():
@@ -99,15 +108,6 @@
         @pl.when(z > 0)
         def _():
             left_copy(q, z, cot.at[0, :, cols(q)]).start()
-
-    def tok_copy(d):
-        k = lax.rem(z + d, n)
-        return pltpu.make_async_remote_copy(
-            src_ref=tok.at[0, :, tok_cols(k)], dst_ref=tokv.at[z], send_sem=tsend.at[d], recv_sem=trecv.at[d],
-            device_id=(me, k), device_id_type=MESH)
-
-    for d in range(1, n):
-        tok_copy(d).start()
 
     def first_leg(c, d):
         j = to(d)

time: 121 us -> 121 us (level)
  no operation moved by 1% of the time
where the time goes in v6:
time: 121 us
  Pallas kernels  120 us (99%)
    pallas_call x1, Pallas kernels, on_device(): pl.pallas_call(functools.partial(kernel, reps, n), out_shape=(pltpu.VMEM(...  117 us
    pallas_call x1, Pallas kernels, on_device(): pl.pallas_call(functools.partial(last_pass, parts), out_shape=(jax.ShapeD...  3.36 us

profile of v6, /device:TPU:0, one launch (start us, length us, event | category | flops | bytes accessed | tf_op | source)
XLA Modules:
  0.0 121.1 jit_solution(15525940104074402728)
XLA Ops:
  0.6 117.1 %shard_map.77 = (bf16[1,1024,2048]{2,1,0:T(8,128)(2,1)S(1)}, f32[1,1024,2048]{2,1,0:T(8,128)S(1)}, f32[1,1024,2048]{2,1,0:T(8,128)S(1)}, f32[1,1,2048]{2,1,0:T(1,128)S(1)}) custom-call(bf16[1,256,4096]{2,1,0:T(8,128)(2,1)} %refs_0_.1, bf16[1,256,2048]{2,1,0:T(8,128)(2,1)} %refs_1_.1, bf16[1,1024,2048]{2,1,0:T(8,128)(2,1)} %refs_2_.1, ...), custom_call_target="tpu_custom_call" | custom-call | flops 4294967296 | bytes 20971520 | tf_op jit(solution)/shard_map/pallas_call | solution.py:382
  117.7 3.4 %shard_map.78 = (bf16[1,1024,2048]{2,1,0:T(8,128)(2,1)}, bf16[1,1024,2048]{2,1,0:T(8,128)(2,1)}) custom-call(bf16[1,1024,2048]{2,1,0:T(8,128)(2,1)S(1)} %get-tuple-element.6.moment, f32[1,1024,2048]{2,1,0:T(8,128)S(1)} %get-tuple-element.7.base, f32[1,1024,2048]{2,1,0:T(8,128)S(1)} %get-tuple-element.8.grad, f32[1,1,2048]{2,1,0:T(1,128)S(1)} %get-tuple-element.9.factor), custom_call_target="tpu_custom_call" | custom-call | flops 4194304 | bytes 8388608 | tf_op jit(solution)/shard_map/pallas_call | solution.py:401

commit v7 on v4

--- a/solution.py
+++ b/solution.py
@@ -8,7 +8,7 @@
 from jax.sharding import PartitionSpec as P
 
 MESH = pl.DeviceIdType.MESH
-CHUNKS = 4
+CHUNKS = 2
 F32 = jnp.float32
 BF16 = jnp.bfloat16
 

time: 121 us -> 122 us (level)
  no operation moved by 1% of the time
where the time goes in v7:
time: 122 us
  Pallas kernels  121 us (99%)
    pallas_call x1, Pallas kernels, on_device(): pl.pallas_call(functools.partial(kernel, reps, n), out_shape=(pltpu.VMEM(...  118 us
    pallas_call x1, Pallas kernels, on_device(): pl.pallas_call(functools.partial(last_pass, parts), out_shape=(jax.ShapeD...  3.36 us

profile of v7, /device:TPU:0, one launch (start us, length us, event | category | flops | bytes accessed | tf_op | source)
XLA Modules:
  0.0 121.8 jit_solution(13238070159829623588)
XLA Ops:
  0.6 117.8 %shard_map.77 = (bf16[1,1024,2048]{2,1,0:T(8,128)(2,1)S(1)}, f32[1,1024,2048]{2,1,0:T(8,128)S(1)}, f32[1,1024,2048]{2,1,0:T(8,128)S(1)}, f32[1,1,2048]{2,1,0:T(1,128)S(1)}) custom-call(bf16[1,256,4096]{2,1,0:T(8,128)(2,1)} %refs_0_.1, bf16[1,256,2048]{2,1,0:T(8,128)(2,1)} %refs_1_.1, bf16[1,1024,2048]{2,1,0:T(8,128)(2,1)} %refs_2_.1, ...), custom_call_target="tpu_custom_call" | custom-call | flops 4294967296 | bytes 20971520 | tf_op jit(solution)/shard_map/pallas_call | solution.py:382
  118.4 3.4 %shard_map.78 = (bf16[1,1024,2048]{2,1,0:T(8,128)(2,1)}, bf16[1,1024,2048]{2,1,0:T(8,128)(2,1)}) custom-call(bf16[1,1024,2048]{2,1,0:T(8,128)(2,1)S(1)} %get-tuple-element.6.moment, f32[1,1024,2048]{2,1,0:T(8,128)S(1)} %get-tuple-element.7.base, f32[1,1024,2048]{2,1,0:T(8,128)S(1)} %get-tuple-element.8.grad, f32[1,1,2048]{2,1,0:T(1,128)S(1)} %get-tuple-element.9.factor), custom_call_target="tpu_custom_call" | custom-call | flops 4194304 | bytes 8388608 | tf_op jit(solution)/shard_map/pallas_call | solution.py:401
